TPU v7x, 32 devices: a whole 2x2x4 slice. The times are simulated.
32 devices in a mesh: member: 4 (over y, x), lat: 8 (over z, core).
Axes of the slice: x: 2, y: 2, z: 4, core: 2. Of those that a mesh axis runs over, the one named last changes fastest.
Arguments:
- states: bfloat16 [4, 16, 256, 256], P('member', 'lat'), may hold values from -6 to 6
- member_id: int32 [4], P('member'), may hold values from 0 to 3, each once
- member_gain: float32 [4, 256], replicated, may hold values from 0.5 to 2
- first_conv: bfloat16 [2304, 256], P('member'), may hold values from -0.125 to 0.125
- second_conv: bfloat16 [2304, 256], P('member'), may hold values from -0.125 to 0.125
- head: bfloat16 [256, 8], replicated, may hold values from -0.375 to 0.375
- target: float32 [8, 16, 256], P(None, 'lat'), may hold values from -6 to 6
- lat_start: int32 [1], replicated, may hold values from 0 to 1785
Outputs:
- score: float32 [8, 16, 256], P(None, 'lat')
- mean_score: float32 [], replicated
All inputs are finite; a program needn't handle non-finite values.
Results may differ from a plain program's by a relative error of at most 0.0018.
Values may be sent and summed in bfloat16 or wider, within the bound.
A program may use at most 64 MiB of HBM per device.

v0:
```python
import jax
import jax.numpy as jnp
from jax import lax
from jax.sharding import PartitionSpec as P


def with_halo(block, sides, width):
    for axis, dim in sides:
        count = lax.axis_size(axis)
        forward = [(i, i + 1) for i in range(count - 1)]
        backward = [(target, source) for source, target in forward]
        low = lax.ppermute(
            lax.slice_in_dim(block, block.shape[dim] - width, None, axis=dim), axis, forward
        )
        high = lax.ppermute(lax.slice_in_dim(block, 0, width, axis=dim), axis, backward)
        block = jnp.concatenate([low, block, high], axis=dim)
    return block


def product(left, right):
    return jnp.dot(
        left.astype(jnp.float32),
        right.astype(jnp.float32),
        precision=lax.Precision.HIGHEST,
        preferred_element_type=jnp.float32,
    )


def patch_rows(field):
    rows, cols, chans = (field.shape[0] - 2, field.shape[1], field.shape[2])
    padded = jnp.pad(field, ((0, 0), (1, 1), (0, 0)))
    taps = [padded[dy : dy + rows, dx : dx + cols, :] for dy in range(3) for dx in range(3)]
    return jnp.concatenate(taps, axis=-1).reshape(rows * cols, 9 * chans)


def folded_conv(patches, weight_rows):
    return product(patches, lax.all_gather(weight_rows, "member", axis=0, tiled=True))


def body(states, member_id, member_gain, first_conv, second_conv, head, target, lat_start):
    rows, cols, chans = (states.shape[1], states.shape[2], states.shape[3])
    members = lax.axis_size("member")
    band = lax.axis_index("lat")
    select = (jnp.arange(members, dtype=jnp.int32)[None, :] == member_id[:, None]).astype(
        jnp.float32
    )
    gain = jnp.dot(select, member_gain, precision=lax.Precision.HIGHEST)
    start = (states[0].astype(jnp.float32) * gain[0]).astype(jnp.bfloat16)

    def with_rims(field):
        return with_halo(field, (("lat", 0),), 1)

    first_out = folded_conv(patch_rows(with_rims(start)), first_conv)
    inner = jax.nn.gelu(first_out, approximate=True).astype(jnp.bfloat16).reshape(rows, cols, -1)
    second_out = folded_conv(patch_rows(with_rims(inner)), second_conv)
    block = (start.reshape(rows * cols, chans).astype(jnp.float32) + second_out).astype(
        jnp.bfloat16
    )
    pred = product(block, head)
    pred = pred.T.reshape(-1, rows, cols).astype(jnp.bfloat16)
    eps = 0.05 / members
    factor = (1.0 - eps) / (2.0 * members * (members - 1))
    fields = lax.all_gather(pred[None], "member", axis=0, tiled=True).astype(jnp.float32)
    skill = jnp.sum(jnp.abs(fields - target[None]), axis=0) / members

    def pair_step(index, total):
        chosen = lax.dynamic_index_in_dim(fields, index, 0, keepdims=True)
        return total + jnp.sum(jnp.abs(chosen - fields), axis=0)

    spread = lax.fori_loop(0, members, pair_step, jnp.zeros_like(skill))
    score = skill - factor * spread
    row_ids = lat_start[0] + band * rows + jnp.arange(rows, dtype=jnp.int32)
    area = jnp.cos(jnp.pi * (90.0 - 0.1 * row_ids.astype(jnp.float32)) / 180.0)
    weighted, area_total = lax.psum((jnp.sum(score * area[None, :, None]), jnp.sum(area)), "lat")
    mean_score = weighted / (score.shape[0] * cols * area_total)
    return (score, mean_score)


def solution(mesh):
    placed = (
        P("member", "lat", None, None),
        P("member"),
        P(),
        P("member", None),
        P("member", None),
        P(),
        P(None, "lat", None),
        P(),
    )
    return jax.shard_map(
        body, mesh=mesh, in_specs=placed, out_specs=(P(None, "lat", None), P()), check_vma=False
    )
```

profile of v0, /device:TPU:0, one launch (start us, length us, event | category | flops | bytes accessed | tf_op | source)
XLA Modules:
  0.0 106.2 jit_solution(5182323818917676973)
XLA Ops:
  7.2 0.0 copy-start
  7.2 0.0 all-gather.3.cloned.1.call-start
  7.2 0.7 all-gather.3.cloned.1.call-update
  7.9 0.0 all-gather.5.cloned.1.call-start
  8.7 0.8 fusion.20
  9.5 1.0 fusion.15
  10.5 2.4 %collective-permute-start = (bf16[1,256,256]{2,1,0:T(8,128)(2,1)S(1)}, bf16[1,256,256]{2,1,0:T(8,128)(2,1)S(1)}, u32[]{:S(2)}, u32[]{:S(2)}) collective-permute-start(bf16[1,256,256]{2,1,0:T(8,128)(2,1)S(1)} %get-tuple-element.107), channel_id=1, source_target_pairs={{0,1},{1,2},{2,3},{3,4},{4,5},{5,6},{6,7},{8,9},{9,10},{10,11},{11... | collective-permute-start | bytes 393224 | tf_op jit(solution)/shard_map/ppermute | solution.py:12
  12.9 1.3 %collective-permute-start.1 = (bf16[1,256,256]{2,1,0:T(8,128)(2,1)S(1)}, bf16[1,256,256]{2,1,0:T(8,128)(2,1)S(1)}, u32[]{:S(2)}, u32[]{:S(2)}) collective-permute-start(bf16[1,256,256]{2,1,0:T(8,128)(2,1)S(1)} %get-tuple-element.108), channel_id=1, source_target_pairs={{1,0},{2,1},{3,2},{4,3},{5,4},{6,5},{7,6},{9,8},{10,9},{11,10},{12... | collective-permute-start | bytes 393224 | tf_op jit(solution)/shard_map/ppermute | solution.py:15
  14.2 0.0 all-gather.5.cloned.1.call-update
  14.2 4.1 %collective-permute-done.1 = bf16[1,256,256]{2,1,0:T(8,128)(2,1)S(1)} collective-permute-done((bf16[1,256,256]{2,1,0:T(8,128)(2,1)S(1)}, bf16[1,256,256]{2,1,0:T(8,128)(2,1)S(1)}, u32[]{:S(2)}, u32[]{:S(2)}) %collective-permute-start.1) | collective-permute-done | bytes 131104 | tf_op jit(solution)/shard_map/ppermute | solution.py:15
  18.3 0.1 fusion.6
  18.5 0.1 slice_dynamic-update-slice_fusion.4
  18.6 0.1 constant_dynamic-update-slice_fusion
  18.7 0.1 slice_dynamic-update-slice_fusion.2
  18.8 0.1 slice_dynamic-update-slice_fusion
  18.9 21.5 %all-gather.3.cloned.1.call-done = bf16[2304,256]{1,0:T(8,128)(2,1)} async-done(((bf16[576,256]{1,0:T(8,128)(2,1)}), bf16[2304,256]{1,0:T(8,128)(2,1)}) %all-gather.3.cloned.1.call-update) | async-done | bytes 1179664 | tf_op jit(solution)/shard_map/all_gather | solution.py:37
  40.3 2.1 %fusion.14 = bf16[512,256]{1,0:T(8,128)(2,1)S(1)} fusion(bf16[512,2304]{1,0:T(8,128)(2,1)S(1)} %bitcast.57, bf16[2304,256]{1,0:T(8,128)(2,1)} %all-gather.3.cloned.1.call-done), kind=kOutput, calls=%fused_computation.24 | convolution fusion | flops 605159424 | bytes 3801088 | tf_op jit(solution)/shard_map/dot_general | solution.py:21
  42.5 1.7 %collective-permute-start.2 = (bf16[1,256,256]{2,1,0:T(8,128)(2,1)S(1)}, bf16[1,256,256]{2,1,0:T(8,128)(2,1)S(1)}, u32[]{:S(2)}, u32[]{:S(2)}) collective-permute-start(bf16[1,256,256]{2,1,0:T(8,128)(2,1)S(1)} %get-tuple-element.105), channel_id=1, source_target_pairs={{0,1},{1,2},{2,3},{3,4},{4,5},{5,6},{6,7},{8,9},{9,10},{10,11},{11... | collective-permute-start | bytes 393224 | tf_op jit(solution)/shard_map/ppermute | solution.py:12
  44.2 1.3 %collective-permute-start.3 = (bf16[1,256,256]{2,1,0:T(8,128)(2,1)S(1)}, bf16[1,256,256]{2,1,0:T(8,128)(2,1)S(1)}, u32[]{:S(2)}, u32[]{:S(2)}) collective-permute-start(bf16[1,256,256]{2,1,0:T(8,128)(2,1)S(1)} %get-tuple-element.106), channel_id=1, source_target_pairs={{1,0},{2,1},{3,2},{4,3},{5,4},{6,5},{7,6},{9,8},{10,9},{11,10},{12... | collective-permute-start | bytes 393224 | tf_op jit(solution)/shard_map/ppermute | solution.py:15
  45.5 0.1 fusion.16
  46.3 0.6 fusion.25
  47.0 1.8 %collective-permute-done.3 = bf16[1,256,256]{2,1,0:T(8,128)(2,1)S(1)} collective-permute-done((bf16[1,256,256]{2,1,0:T(8,128)(2,1)S(1)}, bf16[1,256,256]{2,1,0:T(8,128)(2,1)S(1)}, u32[]{:S(2)}, u32[]{:S(2)}) %collective-permute-start.3) | collective-permute-done | bytes 131104 | tf_op jit(solution)/shard_map/ppermute | solution.py:15
  48.7 0.1 select_maximum_fusion
  48.9 0.2 fusion.27
  49.4 20.5 %all-gather.5.cloned.1.call-done = bf16[2304,256]{1,0:T(8,128)(2,1)} async-done(((bf16[576,256]{1,0:T(8,128)(2,1)}), bf16[2304,256]{1,0:T(8,128)(2,1)}) %all-gather.5.cloned.1.call-update) | async-done | bytes 1179664 | tf_op jit(solution)/shard_map/all_gather | solution.py:37
  69.9 2.0 %fusion = bf16[512,256]{1,0:T(8,128)(2,1)S(1)} fusion(bf16[512,2304]{1,0:T(8,128)(2,1)S(1)} %constant_dynamic-update-slice_fusion.1, bf16[2304,256]{1,0:T(8,128)(2,1)} %all-gather.5.cloned.1.call-done, bf16[512,256]{1,0:T(8,128)(2,1)S(1)} %fusion.16), kind=kOutput, calls=%fused_computation.6 | convolution fusion | flops 604372992 | bytes 4063232 | tf_op jit(solution)/shard_map/dot_general | solution.py:21
  72.0 0.2 convolution_convert_fusion
  72.1 8.1 %all_gather.11 = bf16[4,8,2,256]{3,1,2,0:T(8,128)(2,1)S(1)} all-gather(bf16[1,8,2,256]{3,1,2,0:T(8,128)(2,1)S(1)} %bitcast.56), channel_id=1, replica_groups=mesh['member'=4,'lat'=8] {'member'}, dimensions={0}, use_global_device_ids=true | all-gather | bytes 40960 | tf_op jit(solution)/shard_map/all_gather | solution.py:63
  80.3 0.5 while.14
  80.8 0.7 multiply_reduce_fusion
  81.4 0.6 copy.16
  82.1 15.0 %all-reduce.2 = (f32[]{:T(128)}, f32[]{:T(128)}) all-reduce(f32[]{:T(128)} %get-tuple-element.95, f32[]{:T(128)} %fusion.25), channel_id=1, replica_groups=mesh['member'=4,'lat'=8] {'lat'}, use_global_device_ids=true, to_apply=%region_5.6 | all-reduce | flops 2 | bytes 16 | tf_op jit(solution)/shard_map/psum | solution.py:74
  (41 shorter events, 0.8 us)
Async XLA Ops:
  7.2 64.8 %copy-start = (bf16[256,8]{0,1:T(8,128)(2,1)S(1)}, bf16[256,8]{0,1:T(8,128)(2,1)}, u32[]{:S(2)}) copy-start(bf16[256,8]{0,1:T(8,128)(2,1)} %param.15) | copy-start | bytes 12292
  7.2 33.1 %all-gather.3.cloned.1.call-start = ((), (), s32[]{:S(2)}) async-start(), calls=%async_computation | async-start | bytes 1474560 | tf_op jit(solution)/shard_map/all_gather | solution.py:37
  7.9 10.7 %copy-start.1 = (bf16[1,2,256,256]{3,2,1,0:T(8,128)(2,1)S(1)}, bf16[1,2,256,256]{3,2,1,0:T(8,128)(2,1)}, u32[]{:S(2)}) copy-start(bf16[1,2,256,256]{3,2,1,0:T(8,128)(2,1)} %param.10) | copy-start | bytes 786436
  7.9 62.0 %all-gather.5.cloned.1.call-start = ((), (), s32[]{:S(2)}) async-start(), calls=%async_computation.1 | async-start | bytes 1474560 | tf_op jit(solution)/shard_map/all_gather | solution.py:37
  10.5 3.7 %collective-permute-start = (bf16[1,256,256]{2,1,0:T(8,128)(2,1)S(1)}, bf16[1,256,256]{2,1,0:T(8,128)(2,1)S(1)}, u32[]{:S(2)}, u32[]{:S(2)}) collective-permute-start(bf16[1,256,256]{2,1,0:T(8,128)(2,1)S(1)} %get-tuple-element.107), channel_id=1, source_target_pairs={{0,1},{1,2},{2,3},{3,4},{4,5},{5,6},{6,7},{8,9},{9,10},{10,11},{11... | collective-permute-start | bytes 393224 | tf_op jit(solution)/shard_map/ppermute | solution.py:12
  12.9 5.4 %collective-permute-start.1 = (bf16[1,256,256]{2,1,0:T(8,128)(2,1)S(1)}, bf16[1,256,256]{2,1,0:T(8,128)(2,1)S(1)}, u32[]{:S(2)}, u32[]{:S(2)}) collective-permute-start(bf16[1,256,256]{2,1,0:T(8,128)(2,1)S(1)} %get-tuple-element.108), channel_id=1, source_target_pairs={{1,0},{2,1},{3,2},{4,3},{5,4},{6,5},{7,6},{9,8},{10,9},{11,10},{12... | collective-permute-start | bytes 393224 | tf_op jit(solution)/shard_map/ppermute | solution.py:15
  40.3 5.3 %copy-start.2 = (f32[8,2,256]{2,1,0:T(2,128)S(1)}, f32[8,2,256]{2,1,0:T(2,128)}, u32[]{:S(2)}) copy-start(f32[8,2,256]{2,1,0:T(2,128)} %param.16) | copy-start | bytes 49156
  42.5 4.5 %collective-permute-start.2 = (bf16[1,256,256]{2,1,0:T(8,128)(2,1)S(1)}, bf16[1,256,256]{2,1,0:T(8,128)(2,1)S(1)}, u32[]{:S(2)}, u32[]{:S(2)}) collective-permute-start(bf16[1,256,256]{2,1,0:T(8,128)(2,1)S(1)} %get-tuple-element.105), channel_id=1, source_target_pairs={{0,1},{1,2},{2,3},{3,4},{4,5},{5,6},{6,7},{8,9},{9,10},{10,11},{11... | collective-permute-start | bytes 393224 | tf_op jit(solution)/shard_map/ppermute | solution.py:12
  44.2 4.5 %collective-permute-start.3 = (bf16[1,256,256]{2,1,0:T(8,128)(2,1)S(1)}, bf16[1,256,256]{2,1,0:T(8,128)(2,1)S(1)}, u32[]{:S(2)}, u32[]{:S(2)}) collective-permute-start(bf16[1,256,256]{2,1,0:T(8,128)(2,1)S(1)} %get-tuple-element.106), channel_id=1, source_target_pairs={{1,0},{2,1},{3,2},{4,3},{5,4},{6,5},{7,6},{9,8},{10,9},{11,10},{12... | collective-permute-start | bytes 393224 | tf_op jit(solution)/shard_map/ppermute | solution.py:15
Sparse Core Ops, SparseCore 0:
  9.9 30.4 all-gather.2
  42.2 27.7 all-gather.4
where the time goes:
time: 107 us; the launch traced here: 106 us
  waiting for transfers between devices  48.6 us (45%)
  blocking collectives  23.1 us (22%)
  between operations  18 us (17%)
  starting transfers between devices  6.77 us (6%)
  matrix products  5.13 us (5%)
  other arithmetic  3.14 us (3%)
  local copies, waits for them, and re-layouts  1.34 us (1%)
    all_gather x2, waiting for transfers between devices, folded_conv(): lax.all_gather(weight_rows, 'member', axis=0, tiled=True)  42 us
    psum x1, blocking collectives, body(): lax.psum((jnp.sum(score * area[None, :, None]), jnp.sum(area)), 'lat')  15 us
    all_gather x1, blocking collectives, body(): lax.all_gather(pred[None], 'member', axis=0, tiled=True).astype(jnp.float32)  8.12 us
    ppermute x2, waiting for transfers between devices, with_halo(): lax.ppermute(lax.slice_in_dim(block, 0, width, axis=dim), axis, backward)  5.86 us
    dot_general x3, matrix products, product(): jnp.dot(left.astype(jnp.float32), right.astype(jnp.float32), precision=la...  4.32 us
    ppermute x2, starting transfers between devices, with_halo(): lax.ppermute(lax.slice_in_dim(block, block.shape[dim] - width, None, axis...  4.11 us
    ppermute x2, starting transfers between devices, with_halo(): lax.ppermute(lax.slice_in_dim(block, 0, width, axis=dim), axis, backward)  2.58 us
  transfers between devices with their start and end apart: 6, of which 4 were waited for; matrix products, arithmetic and copies ran while one was open for 5% of the time, Pallas kernels for 0%

commit v1 on v0

v1 whole, which is shorter than its diff:
```python
import functools
import math

import jax
import jax.numpy as jnp
import numpy as np
from jax import lax
from jax.experimental import pallas as pl
from jax.experimental.pallas import tpu as pltpu
from jax.sharding import PartitionSpec as P

MESH = pl.DeviceIdType.MESH
TAPS = 9


def route(members):
    side = math.isqrt(members)
    return (side, side) if side * side == members else (members, 1)


def legs(i1, i2):
    return (i1 > 0) + (i2 > 0)


def tap_plan(members, chans):
    n1, n2 = route(members)
    shard = TAPS * chans // members
    offsets = sorted(
        ((i1, i2) for i1 in range(n1) for i2 in range(n2)), key=lambda o: legs(*o)
    )
    codes, stages = [], []
    for me in range(members):
        for core in range(2):
            u, v = (1 + core * (n1 - 1), n1 - core * (n1 - 1)) if n2 > 1 else (1, members)
            p1, p2 = (me // u) % n1, (me // v) % n2
            arrival = {}
            for stage, (i1, i2) in enumerate(offsets):
                arrival[((p1 - i1) % n1) * u + ((p2 - i2) % n2) * v] = stage
            need = [
                max(
                    arrival[s]
                    for s in range(t * chans // shard, ((t + 1) * chans - 1) // shard + 1)
                )
                for t in range(TAPS)
            ]
            order = sorted(range(TAPS), key=lambda t: need[t])
            codes.append(sum(t * TAPS**i for i, t in enumerate(order)))
            stages.append([need[t] for t in order])
    return offsets, codes, np.max(np.array(stages), axis=0).tolist()


def kernel(
    members, bands, states, ident, gains, w1, w2, head, target, first_row, score_ref, mean_ref,
    raw, sh, ish, wb1, wb2, acc, acc2, preds, parts,
    local_sem, halo_send, halo_recv, leg_send, leg_recv, sib_send, sib_recv,
    pred_send, pred_recv, part_send, part_recv,
):
    rows, cols, chans = states.shape[1:]
    fields = head.shape[1]
    shard = w1.shape[0]
    n1, n2 = route(members)
    offsets, codes, stage_of = tap_plan(members, chans)
    me = lax.axis_index("member")
    lat = lax.axis_index("lat")
    core = lax.rem(lat, 2)
    sibling = lat + 1 - 2 * core

    barrier = pltpu.get_barrier_semaphore()
    for j in range(1, members):
        pl.semaphore_signal(
            barrier, inc=1, device_id=(lax.rem(me + j, members), lat), device_id_type=MESH
        )
    for j in range(1, bands):
        pl.semaphore_signal(
            barrier, inc=1, device_id=(me, lax.rem(lat + j, bands)), device_id_type=MESH
        )

    own_rows = pl.ds(pl.multiple_of(me * shard, 16), shard)
    locals_ = [
        pltpu.make_async_copy(states.at[0], raw.at[pl.ds(rows, rows)], local_sem.at[0]),
        pltpu.make_async_copy(w1, wb1.at[own_rows], local_sem.at[1]),
        pltpu.make_async_copy(w2, wb2.at[own_rows], local_sem.at[2]),
    ]
    for copy in locals_:
        copy.start()

    lane = lax.broadcasted_iota(jnp.int32, gains.shape, 0)
    gain = jnp.sum(jnp.where(lane == ident[0], gains[...], 0.0), axis=0, keepdims=True)

    def area_of(row):
        return jnp.cos(jnp.pi * (90.0 - 0.1 * row) / 180.0)

    start_row = first_row[0]
    all_rows = rows * bands
    width = -(-all_rows // 128) * 128
    ids = lax.broadcasted_iota(jnp.int32, (8, width), 1)
    area_all = area_of((start_row + ids).astype(jnp.float32))
    area_total = jnp.sum(jnp.where(ids < all_rows, area_all, 0.0)[0:1], axis=1, keepdims=True)
    zeros = jnp.zeros((8, 128), jnp.int32)
    areas = [
        area_of((start_row + lat * rows + r + zeros).astype(jnp.float32))[0:1, 0:1]
        for r in range(rows)
    ]
    head_t = head[...].astype(jnp.float32).T.astype(jnp.bfloat16)

    pl.semaphore_wait(barrier, members - 1 + bands - 1)

    if n2 > 1:
        u, v = 1 + core * (n1 - 1), n1 - core * (n1 - 1)
    else:
        u, v = 1, members
    p1 = lax.rem(me // u, n1)
    p2 = lax.rem(me // v, n2)

    def member_at(q1, q2):
        return q1 * u + q2 * v

    def back(i1, i2):
        return member_at(lax.rem(p1 - i1 + n1, n1), lax.rem(p2 - i2 + n2, n2))

    def half(ref, base, which):
        if shard % 32 == 0:
            return ref.at[pl.ds(pl.multiple_of(base + which * (shard // 2), 16), shard // 2)]
        span = ref.shape[1] // 2
        return ref.at[
            pl.ds(pl.multiple_of(base, 16), shard), pl.ds(pl.multiple_of(which * span, 128), span)
        ]

    def leg_copy(w, i1, i2):
        src, buf = ((w1, wb1), (w2, wb2))[w]
        if i2 == 0:
            dest = member_at(lax.rem(p1 + i1, n1), p2)
            origin, j1 = me, 0
        else:
            dest = member_at(p1, lax.rem(p2 + i2, n2))
            origin, j1 = back(i1, 0), i1
        source = half(src, 0, core) if j1 == 0 else half(buf, origin * shard, core)
        return pltpu.make_async_remote_copy(
            src_ref=source,
            dst_ref=half(buf, origin * shard, core),
            send_sem=leg_send.at[w, i1, i2],
            recv_sem=leg_recv.at[w, i1, i2],
            device_id=(dest, lat),
            device_id_type=MESH,
        )

    def sib_copy(w, i1, i2):
        buf = (wb1, wb2)[w]
        place = half(buf, back(i1, i2) * shard, core)
        return pltpu.make_async_remote_copy(
            src_ref=place,
            dst_ref=place,
            send_sem=sib_send.at[w, i1, i2],
            recv_sem=sib_recv.at[w, i1, i2],
            device_id=(me, sibling),
            device_id_type=MESH,
        )

    def send_own(w):
        for i1 in range(1, n1):
            leg_copy(w, i1, 0).start()
        for i2 in range(1, n2):
            leg_copy(w, 0, i2).start()

    def arrive(w, i1, i2):
        leg_copy(w, i1, i2).wait_recv()
        if i2 == 0:
            for j2 in range(1, n2):
                leg_copy(w, i1, j2).start()
        sib_copy(w, i1, i2).start()

    def halo_copy(step):
        place = pl.ds(0, rows) if step > 0 else pl.ds(2 * rows, rows)
        index = 0 if step > 0 else 1
        return pltpu.make_async_remote_copy(
            src_ref=states.at[0],
            dst_ref=raw.at[place],
            send_sem=halo_send.at[index],
            recv_sem=halo_recv.at[index],
            device_id=(me, lat + step),
            device_id_type=MESH,
        )

    has_low, has_high = lat > 0, lat < bands - 1

    @pl.when(has_high)
    def _():
        halo_copy(1).start()

    @pl.when(has_low)
    def _():
        halo_copy(-1).start()

    send_own(0)

    place_ids = lax.broadcasted_iota(jnp.int32, (cols, chans), 0)

    def put_shifted(ref, row, value):
        low = jnp.where(place_ids == 0, 0.0, pltpu.roll(value, 1, 0))
        high = jnp.where(place_ids == cols - 1, 0.0, pltpu.roll(value, cols - 1, 0))
        ref[0, row] = low.astype(jnp.bfloat16)
        ref[1, row] = value.astype(jnp.bfloat16)
        ref[2, row] = high.astype(jnp.bfloat16)

    def scale_rows(first):
        for r in range(rows):
            value = raw[first + r].astype(jnp.float32) * gain
            put_shifted(sh, first + r, value)

    locals_[0].wait()
    scale_rows(rows)

    @pl.when(has_low)
    def _():
        halo_copy(1).wait_recv()

    @pl.when(jnp.logical_not(has_low))
    def _():
        raw[0:rows] = jnp.zeros((rows, cols, chans), jnp.bfloat16)

    @pl.when(has_high)
    def _():
        halo_copy(-1).wait_recv()

    @pl.when(jnp.logical_not(has_high))
    def _():
        raw[2 * rows : 3 * rows] = jnp.zeros((rows, cols, chans), jnp.bfloat16)

    scale_rows(0)
    scale_rows(2 * rows)

    code = jnp.int32(0)
    combo = me * 2 + core
    for index, value in enumerate(codes):
        code = jnp.where(combo == index, jnp.int32(value), code)

    powers = [TAPS**i for i in range(TAPS)]

    def conv(w, field, total, count, base):
        buf = (wb1, wb2)[w]
        for stage, (i1, i2) in enumerate(offsets):
            if stage == 0:
                locals_[1 + w].wait()
            else:
                if legs(i1, i2) > legs(*offsets[stage - 1]):
                    for o1, o2 in offsets:
                        if legs(o1, o2) == legs(i1, i2) and not (w == 0 and o2 == 0):
                            arrive(w, o1, o2)
                sib_copy(w, *((i2, i1) if n2 > 1 else (i1, i2))).wait_recv()
            mine = [i for i in range(TAPS) if stage_of[i] == stage]
            for i in mine:
                tap = lax.rem(code // powers[i], TAPS)
                dy, dx = tap // 3, lax.rem(tap, 3)
                left = field[dx, pl.ds(base + dy, count)].reshape(count * cols, chans)
                right = buf[pl.ds(pl.multiple_of(tap * chans, 128), chans), :]
                term = jnp.dot(left, right, preferred_element_type=jnp.float32)
                if i == 0:
                    total[...] = term
                else:
                    total[...] += term

    for i1 in range(1, n1):
        arrive(0, i1, 0)
    send_own(1)

    conv(0, sh, acc, rows + 2, rows - 2)

    for r in range(rows + 2):
        value = jax.nn.gelu(acc[pl.ds(r * cols, cols), :], approximate=True)
        if r == 0:
            value = jnp.where(has_low, value, 0.0)
        if r == rows + 1:
            value = jnp.where(has_high, value, 0.0)
        put_shifted(ish, r, value)

    conv(1, ish, acc2, rows, 0)

    own = sh[1, pl.ds(rows, rows)].reshape(rows * cols, chans).astype(jnp.float32)
    block = (own + acc2[...]).astype(jnp.bfloat16)
    pred = lax.dot_general(
        head_t, block, (((1,), (1,)), ((), ())), preferred_element_type=jnp.float32
    )
    pred = jnp.concatenate([pred[:, r * cols : (r + 1) * cols] for r in range(rows)], axis=0)
    preds[me] = pred.astype(jnp.bfloat16)

    pred_copies = [
        pltpu.make_async_remote_copy(
            src_ref=preds.at[me],
            dst_ref=preds.at[me],
            send_sem=pred_send.at[j],
            recv_sem=pred_recv.at[j],
            device_id=(lax.rem(me + j, members), lat),
            device_id_type=MESH,
        )
        for j in range(1, members)
    ]
    for copy in pred_copies:
        copy.start()
    for copy in pred_copies:
        copy.wait_recv()

    eps = 0.05 / members
    factor = (1.0 - eps) / (2.0 * members * (members - 1))
    truth = jnp.concatenate([target[:, r, :] for r in range(rows)], axis=0)
    all_preds = [preds[m].astype(jnp.float32) for m in range(members)]
    skill = sum(jnp.abs(p - truth) for p in all_preds) / members
    pairs = sum(
        jnp.abs(all_preds[m] - all_preds[n]) for m in range(members) for n in range(m)
    )
    score = skill - (2.0 * factor) * pairs
    weighted = jnp.zeros((fields, 128), jnp.float32)
    for r in range(rows):
        piece = score[r * fields : (r + 1) * fields]
        score_ref[:, r, :] = piece
        piece = sum(piece[:, c : c + 128] for c in range(0, cols, 128))
        weighted = weighted + piece * areas[r]
    parts[lat] = weighted

    part_copies = [
        pltpu.make_async_remote_copy(
            src_ref=parts.at[lat],
            dst_ref=parts.at[lat],
            send_sem=part_send.at[j],
            recv_sem=part_recv.at[j],
            device_id=(me, lax.rem(lat + j, bands)),
            device_id_type=MESH,
        )
        for j in range(1, bands)
    ]
    for copy in part_copies:
        copy.start()
    for copy in part_copies:
        copy.wait_recv()
    total = jnp.sum(parts[...], axis=0)
    total = jnp.sum(jnp.sum(total, axis=0, keepdims=True), axis=1, keepdims=True)
    mean = total / (fields * cols * area_total)
    mean_ref[0, 0] = mean[0, 0]

    @pl.when(has_high)
    def _():
        halo_copy(1).wait_send()

    @pl.when(has_low)
    def _():
        halo_copy(-1).wait_send()

    for w in range(2):
        for i1, i2 in offsets[1:]:
            leg_copy(w, i1, i2).wait_send()
            sib_copy(w, i1, i2).wait_send()
    for copy in pred_copies + part_copies:
        copy.wait_send()


def body(members, bands, *args):
    states, head = args[0], args[5]
    rows, cols, chans = states.shape[1:]
    fields = head.shape[1]
    n1, n2 = route(members)
    vmem = pl.BlockSpec(memory_space=pltpu.VMEM)
    smem = pl.BlockSpec(memory_space=pltpu.SMEM)
    anywhere = pl.BlockSpec(memory_space=pl.ANY)
    dma = pltpu.SemaphoreType.DMA
    bf16, f32 = jnp.bfloat16, jnp.float32
    score, mean = pl.pallas_call(
        functools.partial(kernel, members, bands),
        out_shape=(
            jax.ShapeDtypeStruct((fields, rows, cols), f32),
            jax.ShapeDtypeStruct((1, 1), f32),
        ),
        in_specs=[anywhere, smem, vmem, anywhere, anywhere, vmem, vmem, smem],
        out_specs=(vmem, smem),
        scratch_shapes=[
            pltpu.VMEM((3 * rows, cols, chans), bf16),
            pltpu.VMEM((3, 3 * rows, cols, chans), bf16),
            pltpu.VMEM((3, rows + 2, cols, chans), bf16),
            pltpu.VMEM((TAPS * chans, chans), bf16),
            pltpu.VMEM((TAPS * chans, chans), bf16),
            pltpu.VMEM(((rows + 2) * cols, chans), f32),
            pltpu.VMEM((rows * cols, chans), f32),
            pltpu.VMEM((members, rows * fields, cols), bf16),
            pltpu.VMEM((bands, fields, 128), f32),
            dma((3,)),
            dma((2,)),
            dma((2,)),
            dma((2, n1, n2)),
            dma((2, n1, n2)),
            dma((2, n1, n2)),
            dma((2, n1, n2)),
            dma((members,)),
            dma((members,)),
            dma((bands,)),
            dma((bands,)),
        ],
        compiler_params=pltpu.CompilerParams(
            collective_id=0, has_side_effects=True, vmem_limit_bytes=40 * 1024 * 1024
        ),
        cost_estimate=pl.CostEstimate(
            flops=2 * 6 * cols * TAPS * chans * chans,
            bytes_accessed=4 * TAPS * chans * chans,
            transcendentals=4 * cols * chans,
        ),
    )(*args)
    return score, mean[0, 0]


def solution(mesh):
    placed = (
        P("member", "lat", None, None),
        P("member"),
        P(),
        P("member", None),
        P("member", None),
        P(),
        P(None, "lat", None),
        P(),
    )
    return jax.shard_map(
        functools.partial(body, mesh.shape["member"], mesh.shape["lat"]),
        mesh=mesh,
        in_specs=placed,
        out_specs=(P(None, "lat", None), P()),
        check_vma=False,
    )
```

time: 107 us -> 38.9 us (0.36)
  waiting for transfers between devices: 48.6 us -> 0 us
  Pallas kernels: 0 us -> 30.7 us
  blocking collectives: 23.1 us -> 0 us
  between operations: 18 us -> 3.66 us
  starting transfers between devices: 6.77 us -> 0 us
  matrix products: 5.13 us -> 0 us
  other arithmetic: 3.14 us -> 0 us
  local copies, waits for them, and re-layouts: 1.34 us -> 4.3 us
    all_gather x2 -> x0, waiting for transfers between devices: 42 us -> none  [folded_conv(): lax.all_gather(weight_rows, 'member', axis=0, tiled=True)]
    pallas_call x0 -> x1, Pallas kernels: none -> 30.7 us  [body(): pl.pallas_call(functools.partial(kernel, members, bands), out_shape=(jax....]
    psum x1 -> x0, blocking collectives: 15 us -> none  [body(): lax.psum((jnp.sum(score * area[None, :, None]), jnp.sum(area)), 'lat')]
    all_gather x1 -> x0, blocking collectives: 8.12 us -> none  [body(): lax.all_gather(pred[None], 'member', axis=0, tiled=True).astype(jnp.float32)]
    ppermute x4 -> x0, starting transfers between devices: 6.7 us -> none  [the longest x2 4.11 us: with_halo(): lax.ppermute(lax.slice_in_dim(block, block.shape[dim] - width, None, axis...]
    ppermute x4 -> x0, waiting for transfers between devices: 5.86 us -> none  [the longest x2 5.86 us: with_halo(): lax.ppermute(lax.slice_in_dim(block, 0, width, axis=dim), axis, backward)]
    dot_general x4 -> x0, matrix products: 5.13 us -> none  [the longest x3 4.32 us: product(): jnp.dot(left.astype(jnp.float32), right.astype(jnp.float32), precision=la...]
    unnamed x22 -> x12, local copies, waits for them, and re-layouts: 1 us -> 4.3 us
  transfers between devices with their start and end apart: 6 -> 0, of which waited for: 4 -> 0; matrix products, arithmetic and copies ran while one was open for 5% -> 0% of each run, Pallas kernels for 0% -> 0%
where the time goes in v1:
time: 38.9 us; the launch traced here: 38.6 us
  Pallas kernels  30.7 us (79%)
  local copies, waits for them, and re-layouts  4.3 us (11%)
  between operations  3.66 us (9%)
    pallas_call x1, Pallas kernels, body(): pl.pallas_call(functools.partial(kernel, members, bands), out_shape=(jax....  30.7 us
    unnamed x12, local copies, waits for them, and re-layouts  4.3 us

profile of v1, /device:TPU:0, one launch (start us, length us, event | category | flops | bytes accessed | tf_op | source)
XLA Modules:
  0.0 38.6 jit_solution(193705301724907210)
XLA Ops:
  1.9 0.0 copy-start.3
  1.9 0.0 copy-start.4
  1.9 0.8 %copy.10.head = bf16[256,8]{1,0:T(8,128)(2,1)S(1)} copy(bf16[256,8]{0,1:T(8,128)(2,1)} %param.13) | data formatting | bytes 8192 | tf_op args[5]
  2.8 0.0 copy-done.3
  2.8 0.0 copy-done.4
  2.8 0.0 copy-start
  2.8 1.0 %copy-done = bf16[576,256]{1,0:T(8,128)(2,1)S(1)} copy-done((bf16[576,256]{1,0:T(8,128)(2,1)S(1)}, bf16[576,256]{1,0:T(8,128)(2,1)}, u32[]{:S(2)}) %copy-start) | copy-done | bytes 294936
  3.7 0.0 copy-start.1
  3.7 1.0 %copy-done.1 = bf16[576,256]{1,0:T(8,128)(2,1)S(1)} copy-done((bf16[576,256]{1,0:T(8,128)(2,1)S(1)}, bf16[576,256]{1,0:T(8,128)(2,1)}, u32[]{:S(2)}) %copy-start.1) | copy-done | bytes 294936
  4.7 0.0 copy-start.2
  4.7 0.9 %copy-done.2 = bf16[1,2,256,256]{3,2,1,0:T(8,128)(2,1)S(1)} copy-done((bf16[1,2,256,256]{3,2,1,0:T(8,128)(2,1)S(1)}, bf16[1,2,256,256]{3,2,1,0:T(8,128)(2,1)}, u32[]{:S(2)}) %copy-start.2) | copy-done | bytes 262168
  5.7 30.7 %shard_map.95 = (f32[8,2,256]{2,1,0:T(2,128)S(1)}, f32[1,1]{1,0:T(1,128)}) custom-call(bf16[1,2,256,256]{3,2,1,0:T(8,128)(2,1)S(1)} %copy-done.2, s32[1]{0:T(128)S(6)} %copy.13.ident, f32[4,256]{1,0:T(4,128)S(1)} %copy-done.4, bf16[576,256]{1,0:T(8,128)(2,1)S(1)} %copy-done, bf16[576,256]{1,0:T(8,128)(2,1)S(1)} %copy-done.1, bf16[256,8]{1,0:T(8,128)(2,1)S(1)} %copy.10.head, ...), custom_call_target="tpu_custom_call" | custom-call | flops 1811939328 | bytes 2359296 | tf_op jit(solution)/shard_map/pallas_call | solution.py:365
  36.3 0.6 %copy.15 = f32[8,2,256]{2,1,0:T(2,128)} copy(f32[8,2,256]{2,1,0:T(2,128)S(1)} %get-tuple-element.8) | data formatting | bytes 32768
Async XLA Ops:
  1.9 0.8 %copy-start.3 = (f32[8,2,256]{2,1,0:T(2,128)S(1)}, f32[8,2,256]{2,1,0:T(2,128)}, u32[]{:S(2)}) copy-start(f32[8,2,256]{2,1,0:T(2,128)} %target.1) | copy-start | bytes 49156
  1.9 0.8 %copy-start.4 = (f32[4,256]{1,0:T(4,128)S(1)}, f32[4,256]{1,0:T(4,128)}, u32[]{:S(2)}) copy-start(f32[4,256]{1,0:T(4,128)} %gains.1) | copy-start | bytes 12292
  2.8 1.0 %copy-start = (bf16[576,256]{1,0:T(8,128)(2,1)S(1)}, bf16[576,256]{1,0:T(8,128)(2,1)}, u32[]{:S(2)}) copy-start(bf16[576,256]{1,0:T(8,128)(2,1)} %w1.1) | copy-start | bytes 884740
  3.7 1.0 %copy-start.1 = (bf16[576,256]{1,0:T(8,128)(2,1)S(1)}, bf16[576,256]{1,0:T(8,128)(2,1)}, u32[]{:S(2)}) copy-start(bf16[576,256]{1,0:T(8,128)(2,1)} %w2.1) | copy-start | bytes 884740
  4.7 0.9 %copy-start.2 = (bf16[1,2,256,256]{3,2,1,0:T(8,128)(2,1)S(1)}, bf16[1,2,256,256]{3,2,1,0:T(8,128)(2,1)}, u32[]{:S(2)}) copy-start(bf16[1,2,256,256]{3,2,1,0:T(8,128)(2,1)} %states.1) | copy-start | bytes 786436

commit v2 on v1

--- a/solution.py
+++ b/solution.py
@@ -50,13 +50,13 @@
 
 
 def kernel(
-    members, bands, states, ident, gains, w1, w2, head, target, first_row, score_ref, mean_ref,
-    raw, sh, ish, wb1, wb2, acc, acc2, preds, parts,
+    members, bands, states, ident_hbm, gains_hbm, w1, w2, head_hbm, target_hbm, first_row_hbm,
+    score_ref, mean_ref, ident, gains, head, target, first_row, raw, sh, ish, wb1, wb2, acc, acc2, preds, parts,
     local_sem, halo_send, halo_recv, leg_send, leg_recv, sib_send, sib_recv,
     pred_send, pred_recv, part_send, part_recv,
 ):
     rows, cols, chans = states.shape[1:]
-    fields = head.shape[1]
+    fields = head_hbm.shape[0]
     shard = w1.shape[0]
     n1, n2 = route(members)
     offsets, codes, stage_of = tap_plan(members, chans)
@@ -81,8 +81,22 @@
         pltpu.make_async_copy(w1, wb1.at[own_rows], local_sem.at[1]),
         pltpu.make_async_copy(w2, wb2.at[own_rows], local_sem.at[2]),
     ]
-    for copy in locals_:
+    small = [
+        pltpu.make_async_copy(source, place, local_sem.at[3 + index])
+        for index, (source, place) in enumerate(
+            (
+                (ident_hbm, ident),
+                (gains_hbm, gains),
+                (first_row_hbm, first_row),
+                (head_hbm, head),
+                (target_hbm, target),
+            )
+        )
+    ]
+    for copy in small + locals_:
         copy.start()
+    for copy in small:
+        copy.wait()
 
     lane = lax.broadcasted_iota(jnp.int32, gains.shape, 0)
     gain = jnp.sum(jnp.where(lane == ident[0], gains[...], 0.0), axis=0, keepdims=True)
@@ -101,7 +115,23 @@
         area_of((start_row + lat * rows + r + zeros).astype(jnp.float32))[0:1, 0:1]
         for r in range(rows)
     ]
-    head_t = head[...].astype(jnp.float32).T.astype(jnp.bfloat16)
+
+    place_ids = lax.broadcasted_iota(jnp.int32, (cols, chans), 0)
+
+    def put_shifted(ref, row, value):
+        low = jnp.where(place_ids == 0, 0.0, pltpu.roll(value, 1, 0))
+        high = jnp.where(place_ids == cols - 1, 0.0, pltpu.roll(value, cols - 1, 0))
+        ref[0, row] = low.astype(jnp.bfloat16)
+        ref[1, row] = value.astype(jnp.bfloat16)
+        ref[2, row] = high.astype(jnp.bfloat16)
+
+    def scale_rows(first):
+        for r in range(rows):
+            value = raw[first + r].astype(jnp.float32) * gain
+            put_shifted(sh, first + r, value)
+
+    locals_[0].wait()
+    scale_rows(rows)
 
     pl.semaphore_wait(barrier, members - 1 + bands - 1)
 
@@ -181,6 +211,7 @@
             device_id_type=MESH,
         )
 
+    send_own(0)
     has_low, has_high = lat > 0, lat < bands - 1
 
     @pl.when(has_high)
@@ -191,24 +222,10 @@
     def _():
         halo_copy(-1).start()
 
-    send_own(0)
-
-    place_ids = lax.broadcasted_iota(jnp.int32, (cols, chans), 0)
-
-    def put_shifted(ref, row, value):
-        low = jnp.where(place_ids == 0, 0.0, pltpu.roll(value, 1, 0))
-        high = jnp.where(place_ids == cols - 1, 0.0, pltpu.roll(value, cols - 1, 0))
-        ref[0, row] = low.astype(jnp.bfloat16)
-        ref[1, row] = value.astype(jnp.bfloat16)
-        ref[2, row] = high.astype(jnp.bfloat16)
-
-    def scale_rows(first):
-        for r in range(rows):
-            value = raw[first + r].astype(jnp.float32) * gain
-            put_shifted(sh, first + r, value)
-
-    locals_[0].wait()
-    scale_rows(rows)
+    for i1 in range(1, n1):
+        arrive(0, i1, 0)
+    send_own(1)
+
 
     @pl.when(has_low)
     def _():
@@ -259,10 +276,6 @@
                 else:
                     total[...] += term
 
-    for i1 in range(1, n1):
-        arrive(0, i1, 0)
-    send_own(1)
-
     conv(0, sh, acc, rows + 2, rows - 2)
 
     for r in range(rows + 2):
@@ -278,7 +291,7 @@
     own = sh[1, pl.ds(rows, rows)].reshape(rows * cols, chans).astype(jnp.float32)
     block = (own + acc2[...]).astype(jnp.bfloat16)
     pred = lax.dot_general(
-        head_t, block, (((1,), (1,)), ((), ())), preferred_element_type=jnp.float32
+        head[...], block, (((1,), (1,)), ((), ())), preferred_element_type=jnp.float32
     )
     pred = jnp.concatenate([pred[:, r * cols : (r + 1) * cols] for r in range(rows)], axis=0)
     preds[me] = pred.astype(jnp.bfloat16)
@@ -356,10 +369,11 @@
     states, head = args[0], args[5]
     rows, cols, chans = states.shape[1:]
     fields = head.shape[1]
+    args = args[:5] + (head.T,) + args[6:]
     n1, n2 = route(members)
+    hbm = pl.BlockSpec(memory_space=pltpu.HBM)
     vmem = pl.BlockSpec(memory_space=pltpu.VMEM)
     smem = pl.BlockSpec(memory_space=pltpu.SMEM)
-    anywhere = pl.BlockSpec(memory_space=pl.ANY)
     dma = pltpu.SemaphoreType.DMA
     bf16, f32 = jnp.bfloat16, jnp.float32
     score, mean = pl.pallas_call(
@@ -368,9 +382,14 @@
             jax.ShapeDtypeStruct((fields, rows, cols), f32),
             jax.ShapeDtypeStruct((1, 1), f32),
         ),
-        in_specs=[anywhere, smem, vmem, anywhere, anywhere, vmem, vmem, smem],
+        in_specs=[hbm] * 8,
         out_specs=(vmem, smem),
         scratch_shapes=[
+            pltpu.SMEM((1,), jnp.int32),
+            pltpu.VMEM(args[2].shape, f32),
+            pltpu.VMEM((fields, chans), bf16),
+            pltpu.VMEM(args[6].shape, f32),
+            pltpu.SMEM((1,), jnp.int32),
             pltpu.VMEM((3 * rows, cols, chans), bf16),
             pltpu.VMEM((3, 3 * rows, cols, chans), bf16),
             pltpu.VMEM((3, rows + 2, cols, chans), bf16),
@@ -380,7 +399,7 @@
             pltpu.VMEM((rows * cols, chans), f32),
             pltpu.VMEM((members, rows * fields, cols), bf16),
             pltpu.VMEM((bands, fields, 128), f32),
-            dma((3,)),
+            dma((8,)),
             dma((2,)),
             dma((2,)),
             dma((2, n1, n2)),
@@ -393,7 +412,7 @@
             dma((bands,)),
         ],
         compiler_params=pltpu.CompilerParams(
-            collective_id=0, has_side_effects=True, vmem_limit_bytes=40 * 1024 * 1024
+            collective_id=0, has_side_effects=True, vmem_limit_bytes=62 * 1024 * 1024
         ),
         cost_estimate=pl.CostEstimate(
             flops=2 * 6 * cols * TAPS * chans * chans,

time: 38.9 us -> 35.7 us (0.918)
  local copies, waits for them, and re-layouts: 4.3 us -> 1.32 us
    unnamed x12 -> x1, local copies, waits for them, and re-layouts: 4.3 us -> 1.32 us
where the time goes in v2:
time: 35.7 us; the launch traced here: 35.4 us
  Pallas kernels  30.4 us (85%)
  between operations  3.7 us (10%)
  local copies, waits for them, and re-layouts  1.32 us (4%)
    pallas_call x1, Pallas kernels, body(): pl.pallas_call(functools.partial(kernel, members, bands), out_shape=(jax....  30.4 us
    unnamed x1, local copies, waits for them, and re-layouts  1.32 us

profile of v2, /device:TPU:0, one launch (start us, length us, event | category | flops | bytes accessed | tf_op | source)
XLA Modules:
  0.0 35.4 jit_solution(3340753939745016327)
XLA Ops:
  1.9 30.4 %shard_map.95 = (f32[8,2,256]{2,1,0:T(2,128)}, f32[1,1]{1,0:T(1,128)}) custom-call(bf16[1,2,256,256]{3,2,1,0:T(8,128)(2,1)} %states.1, s32[1]{0:T(128)S(6)} %copy.12.ident_hbm, f32[4,256]{1,0:T(4,128)} %gains_hbm.1, bf16[576,256]{1,0:T(8,128)(2,1)} %w1.1, bf16[576,256]{1,0:T(8,128)(2,1)} %w2.1, bf16[8,256]{1,0:T(8,128)(2,1)} %bitcast.2, ...), custom_call_target="tpu_custom_call" | custom-call | flops 1811939328 | bytes 2359296 | tf_op jit(solution)/shard_map/pallas_call | solution.py:379
  32.3 1.3 %copy.14 = f32[8,2,256]{2,1,0:T(2,128)} copy(f32[8,2,256]{2,1,0:T(2,128)} %get-tuple-element.8) | data formatting | bytes 32768

commit v3 on v2

--- a/solution.py
+++ b/solution.py
@@ -49,6 +49,10 @@
     return offsets, codes, np.max(np.array(stages), axis=0).tolist()
 
 
+def chunk_count(shard):
+    return 2 if shard % 64 == 0 else 1
+
+
 def kernel(
     members, bands, states, ident_hbm, gains_hbm, w1, w2, head_hbm, target_hbm, first_row_hbm,
     score_ref, mean_ref, ident, gains, head, target, first_row, raw, sh, ish, wb1, wb2, acc, acc2, preds, parts,
@@ -148,15 +152,19 @@
     def back(i1, i2):
         return member_at(lax.rem(p1 - i1 + n1, n1), lax.rem(p2 - i2 + n2, n2))
 
-    def half(ref, base, which):
-        if shard % 32 == 0:
-            return ref.at[pl.ds(pl.multiple_of(base + which * (shard // 2), 16), shard // 2)]
+    chunks = chunk_count(shard)
+
+    def half(ref, base, which, chunk):
+        if shard % (32 * chunks) == 0:
+            size = shard // (2 * chunks)
+            first = base + which * (shard // 2) + chunk * size
+            return ref.at[pl.ds(pl.multiple_of(first, 16), size)]
         span = ref.shape[1] // 2
         return ref.at[
             pl.ds(pl.multiple_of(base, 16), shard), pl.ds(pl.multiple_of(which * span, 128), span)
         ]
 
-    def leg_copy(w, i1, i2):
+    def leg_copy(w, i1, i2, chunk):
         src, buf = ((w1, wb1), (w2, wb2))[w]
         if i2 == 0:
             dest = member_at(lax.rem(p1 + i1, n1), p2)
@@ -164,40 +172,44 @@
         else:
             dest = member_at(p1, lax.rem(p2 + i2, n2))
             origin, j1 = back(i1, 0), i1
-        source = half(src, 0, core) if j1 == 0 else half(buf, origin * shard, core)
+        source = (
+            half(src, 0, core, chunk) if j1 == 0 else half(buf, origin * shard, core, chunk)
+        )
         return pltpu.make_async_remote_copy(
             src_ref=source,
-            dst_ref=half(buf, origin * shard, core),
-            send_sem=leg_send.at[w, i1, i2],
-            recv_sem=leg_recv.at[w, i1, i2],
+            dst_ref=half(buf, origin * shard, core, chunk),
+            send_sem=leg_send.at[w, i1, i2, chunk],
+            recv_sem=leg_recv.at[w, i1, i2, chunk],
             device_id=(dest, lat),
             device_id_type=MESH,
         )
 
-    def sib_copy(w, i1, i2):
+    def sib_copy(w, i1, i2, chunk):
         buf = (wb1, wb2)[w]
-        place = half(buf, back(i1, i2) * shard, core)
+        place = half(buf, back(i1, i2) * shard, core, chunk)
         return pltpu.make_async_remote_copy(
             src_ref=place,
             dst_ref=place,
-            send_sem=sib_send.at[w, i1, i2],
-            recv_sem=sib_recv.at[w, i1, i2],
+            send_sem=sib_send.at[w, i1, i2, chunk],
+            recv_sem=sib_recv.at[w, i1, i2, chunk],
             device_id=(me, sibling),
             device_id_type=MESH,
         )
 
     def send_own(w):
-        for i1 in range(1, n1):
-            leg_copy(w, i1, 0).start()
-        for i2 in range(1, n2):
-            leg_copy(w, 0, i2).start()
+        for chunk in range(chunks):
+            for i1 in range(1, n1):
+                leg_copy(w, i1, 0, chunk).start()
+            for i2 in range(1, n2):
+                leg_copy(w, 0, i2, chunk).start()
 
     def arrive(w, i1, i2):
-        leg_copy(w, i1, i2).wait_recv()
-        if i2 == 0:
-            for j2 in range(1, n2):
-                leg_copy(w, i1, j2).start()
-        sib_copy(w, i1, i2).start()
+        for chunk in range(chunks):
+            leg_copy(w, i1, i2, chunk).wait_recv()
+            if i2 == 0:
+                for j2 in range(1, n2):
+                    leg_copy(w, i1, j2, chunk).start()
+            sib_copy(w, i1, i2, chunk).start()
 
     def halo_copy(step):
         place = pl.ds(0, rows) if step > 0 else pl.ds(2 * rows, rows)
@@ -261,9 +273,10 @@
             else:
                 if legs(i1, i2) > legs(*offsets[stage - 1]):
                     for o1, o2 in offsets:
-                        if legs(o1, o2) == legs(i1, i2) and not (w == 0 and o2 == 0):
+                        if legs(o1, o2) == legs(i1, i2) and o2 > 0:
                             arrive(w, o1, o2)
-                sib_copy(w, *((i2, i1) if n2 > 1 else (i1, i2))).wait_recv()
+                for chunk in range(chunks):
+                    sib_copy(w, *((i2, i1) if n2 > 1 else (i1, i2)), chunk).wait_recv()
             mine = [i for i in range(TAPS) if stage_of[i] == stage]
             for i in mine:
                 tap = lax.rem(code // powers[i], TAPS)
@@ -277,6 +290,9 @@
                     total[...] += term
 
     conv(0, sh, acc, rows + 2, rows - 2)
+
+    for i1 in range(1, n1):
+        arrive(1, i1, 0)
 
     for r in range(rows + 2):
         value = jax.nn.gelu(acc[pl.ds(r * cols, cols), :], approximate=True)
@@ -359,8 +375,9 @@
 
     for w in range(2):
         for i1, i2 in offsets[1:]:
-            leg_copy(w, i1, i2).wait_send()
-            sib_copy(w, i1, i2).wait_send()
+            for chunk in range(chunks):
+                leg_copy(w, i1, i2, chunk).wait_send()
+                sib_copy(w, i1, i2, chunk).wait_send()
     for copy in pred_copies + part_copies:
         copy.wait_send()
 
@@ -371,6 +388,7 @@
     fields = head.shape[1]
     args = args[:5] + (head.T,) + args[6:]
     n1, n2 = route(members)
+    chunks = chunk_count(args[3].shape[0])
     hbm = pl.BlockSpec(memory_space=pltpu.HBM)
     vmem = pl.BlockSpec(memory_space=pltpu.VMEM)
     smem = pl.BlockSpec(memory_space=pltpu.SMEM)
@@ -402,10 +420,10 @@
             dma((8,)),
             dma((2,)),
             dma((2,)),
-            dma((2, n1, n2)),
-            dma((2, n1, n2)),
-            dma((2, n1, n2)),
-            dma((2, n1, n2)),
+            dma((2, n1, n2, chunks)),
+            dma((2, n1, n2, chunks)),
+            dma((2, n1, n2, chunks)),
+            dma((2, n1, n2, chunks)),
             dma((members,)),
             dma((members,)),
             dma((bands,)),

time: 35.7 us -> 35.1 us (0.983)
  Pallas kernels: 30.4 us -> 29.8 us
    pallas_call x1, Pallas kernels: 30.4 us -> 29.8 us  [body(): pl.pallas_call(functools.partial(kernel, members, bands), out_shape=(jax....]
where the time goes in v3:
time: 35.1 us; the launch traced here: 34.8 us
  Pallas kernels  29.8 us (85%)
  between operations  3.7 us (11%)
  local copies, waits for them, and re-layouts  1.32 us (4%)
    pallas_call x1, Pallas kernels, body(): pl.pallas_call(functools.partial(kernel, members, bands), out_shape=(jax....  29.8 us
    unnamed x1, local copies, waits for them, and re-layouts  1.32 us

profile of v3, /device:TPU:0, one launch (start us, length us, event | category | flops | bytes accessed | tf_op | source)
XLA Modules:
  0.0 34.8 jit_solution(8902424833396013106)
XLA Ops:
  1.9 29.8 %shard_map.95 = (f32[8,2,256]{2,1,0:T(2,128)}, f32[1,1]{1,0:T(1,128)}) custom-call(bf16[1,2,256,256]{3,2,1,0:T(8,128)(2,1)} %states.1, s32[1]{0:T(128)S(6)} %copy.12.ident_hbm, f32[4,256]{1,0:T(4,128)} %gains_hbm.1, bf16[576,256]{1,0:T(8,128)(2,1)} %w1.1, bf16[576,256]{1,0:T(8,128)(2,1)} %w2.1, bf16[8,256]{1,0:T(8,128)(2,1)} %bitcast.2, ...), custom_call_target="tpu_custom_call" | custom-call | flops 1811939328 | bytes 2359296 | tf_op jit(solution)/shard_map/pallas_call | solution.py:397
  31.7 1.3 %copy.14 = f32[8,2,256]{2,1,0:T(2,128)} copy(f32[8,2,256]{2,1,0:T(2,128)} %get-tuple-element.8) | data formatting | bytes 32768

commit v4 on v3

--- a/solution.py
+++ b/solution.py
@@ -55,7 +55,7 @@
 
 def kernel(
     members, bands, states, ident_hbm, gains_hbm, w1, w2, head_hbm, target_hbm, first_row_hbm,
-    score_ref, mean_ref, ident, gains, head, target, first_row, raw, sh, ish, wb1, wb2, acc, acc2, preds, parts,
+    score_ref, mean_ref, ident, gains, head, target, first_row, gain_ref, raw, sh, ish, wb1, wb2, acc, acc2, preds, parts,
     local_sem, halo_send, halo_recv, leg_send, leg_recv, sib_send, sib_recv,
     pred_send, pred_recv, part_send, part_recv,
 ):
@@ -105,37 +105,43 @@
     lane = lax.broadcasted_iota(jnp.int32, gains.shape, 0)
     gain = jnp.sum(jnp.where(lane == ident[0], gains[...], 0.0), axis=0, keepdims=True)
 
-    def area_of(row):
-        return jnp.cos(jnp.pi * (90.0 - 0.1 * row) / 180.0)
-
-    start_row = first_row[0]
     all_rows = rows * bands
     width = -(-all_rows // 128) * 128
     ids = lax.broadcasted_iota(jnp.int32, (8, width), 1)
-    area_all = area_of((start_row + ids).astype(jnp.float32))
-    area_total = jnp.sum(jnp.where(ids < all_rows, area_all, 0.0)[0:1], axis=1, keepdims=True)
-    zeros = jnp.zeros((8, 128), jnp.int32)
-    areas = [
-        area_of((start_row + lat * rows + r + zeros).astype(jnp.float32))[0:1, 0:1]
-        for r in range(rows)
-    ]
-
-    place_ids = lax.broadcasted_iota(jnp.int32, (cols, chans), 0)
-
-    def put_shifted(ref, row, value):
+    area_all = jnp.cos(jnp.pi * (90.0 - 0.1 * (first_row[0] + ids).astype(jnp.float32)) / 180.0)
+
+    def area_sum(chosen):
+        return jnp.sum(jnp.where(chosen, area_all, 0.0)[0:1], axis=1, keepdims=True)
+
+    area_total = area_sum(ids < all_rows)
+    areas = [area_sum(ids == lat * rows + r) for r in range(rows)]
+
+    strip = 128
+    strips = chans // strip
+    place_ids = lax.broadcasted_iota(jnp.int32, (cols, strip), 0)
+
+    def lanes_of(index):
+        return pl.ds(pl.multiple_of(lax.rem(index, strips) * strip, strip), strip)
+
+    def put_shifted(ref, row, lanes, value):
         low = jnp.where(place_ids == 0, 0.0, pltpu.roll(value, 1, 0))
         high = jnp.where(place_ids == cols - 1, 0.0, pltpu.roll(value, cols - 1, 0))
-        ref[0, row] = low.astype(jnp.bfloat16)
-        ref[1, row] = value.astype(jnp.bfloat16)
-        ref[2, row] = high.astype(jnp.bfloat16)
-
-    def scale_rows(first):
-        for r in range(rows):
-            value = raw[first + r].astype(jnp.float32) * gain
-            put_shifted(sh, first + r, value)
-
+        ref[0, row, :, lanes] = low.astype(jnp.bfloat16)
+        ref[1, row, :, lanes] = value.astype(jnp.bfloat16)
+        ref[2, row, :, lanes] = high.astype(jnp.bfloat16)
+
+    def scale_rows(count, place):
+        @pl.loop(0, count * strips)
+        def _(index):
+            row, lanes = place(index // strips), lanes_of(index)
+            value = raw[row, :, lanes].astype(jnp.float32) * gain_ref[0:1, lanes]
+            put_shifted(sh, row, lanes, value)
+
+    gain_ref[...] = jnp.broadcast_to(gain, gain_ref.shape)
     locals_[0].wait()
-    scale_rows(rows)
+    scale_rows(rows, lambda r: r + rows)
+    acc[...] = jnp.zeros_like(acc)
+    acc2[...] = jnp.zeros_like(acc2)
 
     pl.semaphore_wait(barrier, members - 1 + bands - 1)
 
@@ -255,52 +261,63 @@
     def _():
         raw[2 * rows : 3 * rows] = jnp.zeros((rows, cols, chans), jnp.bfloat16)
 
-    scale_rows(0)
-    scale_rows(2 * rows)
+    scale_rows(2 * rows, lambda r: r + rows * (r // rows))
 
     code = jnp.int32(0)
     combo = me * 2 + core
     for index, value in enumerate(codes):
         code = jnp.where(combo == index, jnp.int32(value), code)
 
-    powers = [TAPS**i for i in range(TAPS)]
+    def stage_waits(w, stage):
+        i1, i2 = offsets[stage]
+        if stage == 0:
+            locals_[1 + w].wait()
+            return
+        if legs(i1, i2) > legs(*offsets[stage - 1]):
+            for o1, o2 in offsets:
+                if legs(o1, o2) == legs(i1, i2) and o2 > 0:
+                    arrive(w, o1, o2)
+        for chunk in range(chunks):
+            sib_copy(w, *((i2, i1) if n2 > 1 else (i1, i2)), chunk).wait_recv()
 
     def conv(w, field, total, count, base):
         buf = (wb1, wb2)[w]
-        for stage, (i1, i2) in enumerate(offsets):
-            if stage == 0:
-                locals_[1 + w].wait()
-            else:
-                if legs(i1, i2) > legs(*offsets[stage - 1]):
-                    for o1, o2 in offsets:
-                        if legs(o1, o2) == legs(i1, i2) and o2 > 0:
-                            arrive(w, o1, o2)
-                for chunk in range(chunks):
-                    sib_copy(w, *((i2, i1) if n2 > 1 else (i1, i2)), chunk).wait_recv()
-            mine = [i for i in range(TAPS) if stage_of[i] == stage]
-            for i in mine:
-                tap = lax.rem(code // powers[i], TAPS)
-                dy, dx = tap // 3, lax.rem(tap, 3)
-                left = field[dx, pl.ds(base + dy, count)].reshape(count * cols, chans)
-                right = buf[pl.ds(pl.multiple_of(tap * chans, 128), chans), :]
-                term = jnp.dot(left, right, preferred_element_type=jnp.float32)
-                if i == 0:
-                    total[...] = term
-                else:
-                    total[...] += term
+
+        def step(i, left_code):
+            done = 0
+            for at in range(TAPS):
+                due = list(range(done, stage_of[at] + 1))
+                done = max(done, stage_of[at] + 1)
+                if due:
+
+                    @pl.when(i == at)
+                    def _():
+                        for stage in due:
+                            stage_waits(w, stage)
+
+            tap = lax.rem(left_code, TAPS)
+            dy, dx = tap // 3, lax.rem(tap, 3)
+            left = field[dx, pl.ds(base + dy, count)].reshape(count * cols, chans)
+            right = buf[pl.ds(pl.multiple_of(tap * chans, 128), chans), :]
+            total[...] += jnp.dot(left, right, preferred_element_type=jnp.float32)
+            return left_code // TAPS
+
+        lax.fori_loop(0, TAPS, step, code)
 
     conv(0, sh, acc, rows + 2, rows - 2)
 
     for i1 in range(1, n1):
         arrive(1, i1, 0)
 
-    for r in range(rows + 2):
-        value = jax.nn.gelu(acc[pl.ds(r * cols, cols), :], approximate=True)
-        if r == 0:
-            value = jnp.where(has_low, value, 0.0)
-        if r == rows + 1:
-            value = jnp.where(has_high, value, 0.0)
-        put_shifted(ish, r, value)
+    @pl.loop(0, (rows + 2) * strips)
+    def _(index):
+        row, lanes = index // strips, lanes_of(index)
+        at = pl.ds(pl.multiple_of(row * cols, cols), cols)
+        value = jax.nn.gelu(acc[at, lanes], approximate=True)
+        inside = jnp.logical_and(
+            jnp.logical_or(row > 0, has_low), jnp.logical_or(row < rows + 1, has_high)
+        )
+        put_shifted(ish, row, lanes, jnp.where(inside, value, 0.0))
 
     conv(1, ish, acc2, rows, 0)
 
@@ -408,6 +425,7 @@
             pltpu.VMEM((fields, chans), bf16),
             pltpu.VMEM(args[6].shape, f32),
             pltpu.SMEM((1,), jnp.int32),
+            pltpu.VMEM((8, chans), f32),
             pltpu.VMEM((3 * rows, cols, chans), bf16),
             pltpu.VMEM((3, 3 * rows, cols, chans), bf16),
             pltpu.VMEM((3, rows + 2, cols, chans), bf16),

time: 35.1 us -> 35.7 us (1.017)
  Pallas kernels: 29.8 us -> 30.3 us
    pallas_call x1, Pallas kernels: 29.8 us -> 30.3 us  [body(): pl.pallas_call(functools.partial(kernel, members, bands), out_shape=(jax....]
where the time goes in v4:
time: 35.7 us; the launch traced here: 35.4 us
  Pallas kernels  30.3 us (85%)
  between operations  3.7 us (10%)
  local copies, waits for them, and re-layouts  1.32 us (4%)
    pallas_call x1, Pallas kernels, body(): pl.pallas_call(functools.partial(kernel, members, bands), out_shape=(jax....  30.3 us
    unnamed x1, local copies, waits for them, and re-layouts  1.32 us

profile of v4, /device:TPU:0, one launch (start us, length us, event | category | flops | bytes accessed | tf_op | source)
XLA Modules:
  0.0 35.4 jit_solution(18138924164440107202)
XLA Ops:
  1.9 30.3 %shard_map.95 = (f32[8,2,256]{2,1,0:T(2,128)}, f32[1,1]{1,0:T(1,128)}) custom-call(bf16[1,2,256,256]{3,2,1,0:T(8,128)(2,1)} %states.1, s32[1]{0:T(128)S(6)} %copy.12.ident_hbm, f32[4,256]{1,0:T(4,128)} %gains_hbm.1, bf16[576,256]{1,0:T(8,128)(2,1)} %w1.1, bf16[576,256]{1,0:T(8,128)(2,1)} %w2.1, bf16[8,256]{1,0:T(8,128)(2,1)} %bitcast.2, ...), custom_call_target="tpu_custom_call" | custom-call | flops 1811939328 | bytes 2359296 | tf_op jit(solution)/shard_map/pallas_call | solution.py:414
  32.3 1.3 %copy.14 = f32[8,2,256]{2,1,0:T(2,128)} copy(f32[8,2,256]{2,1,0:T(2,128)} %get-tuple-element.8) | data formatting | bytes 32768

commit v5 on v4

--- a/solution.py
+++ b/solution.py
@@ -202,15 +202,15 @@
             device_id_type=MESH,
         )
 
-    def send_own(w):
-        for chunk in range(chunks):
+    def send_own(w, some):
+        for chunk in some:
             for i1 in range(1, n1):
                 leg_copy(w, i1, 0, chunk).start()
             for i2 in range(1, n2):
                 leg_copy(w, 0, i2, chunk).start()
 
-    def arrive(w, i1, i2):
-        for chunk in range(chunks):
+    def arrive(w, i1, i2, some=range(chunks)):
+        for chunk in some:
             leg_copy(w, i1, i2, chunk).wait_recv()
             if i2 == 0:
                 for j2 in range(1, n2):
@@ -229,7 +229,7 @@
             device_id_type=MESH,
         )
 
-    send_own(0)
+    send_own(0, range(chunks))
     has_low, has_high = lat > 0, lat < bands - 1
 
     @pl.when(has_high)
@@ -240,9 +240,10 @@
     def _():
         halo_copy(-1).start()
 
-    for i1 in range(1, n1):
-        arrive(0, i1, 0)
-    send_own(1)
+    for chunk in range(chunks):
+        for i1 in range(1, n1):
+            arrive(0, i1, 0, [chunk])
+        send_own(1, [chunk])
 
 
     @pl.when(has_low)
@@ -274,6 +275,9 @@
             locals_[1 + w].wait()
             return
         if legs(i1, i2) > legs(*offsets[stage - 1]):
+            if w == 0 and legs(i1, i2) == 2:
+                for o1 in range(1, n1):
+                    arrive(1, o1, 0)
             for o1, o2 in offsets:
                 if legs(o1, o2) == legs(i1, i2) and o2 > 0:
                     arrive(w, o1, o2)
@@ -303,12 +307,11 @@
             return left_code // TAPS
 
         lax.fori_loop(0, TAPS, step, code)
+        if w == 0 and n2 == 1:
+            for o1 in range(1, n1):
+                arrive(1, o1, 0)
 
     conv(0, sh, acc, rows + 2, rows - 2)
-
-    for i1 in range(1, n1):
-        arrive(1, i1, 0)
-
     @pl.loop(0, (rows + 2) * strips)
     def _(index):
         row, lanes = index // strips, lanes_of(index)

time: 35.7 us -> 35.4 us (level)
  no operation moved by 1% of the time
where the time goes in v5:
time: 35.4 us; the launch traced here: 35.1 us
  Pallas kernels  30 us (85%)
  between operations  3.7 us (10%)
  local copies, waits for them, and re-layouts  1.32 us (4%)
    pallas_call x1, Pallas kernels, body(): pl.pallas_call(functools.partial(kernel, members, bands), out_shape=(jax....  30 us
    unnamed x1, local copies, waits for them, and re-layouts  1.32 us

profile of v5, /device:TPU:0, one launch (start us, length us, event | category | flops | bytes accessed | tf_op | source)
XLA Modules:
  0.0 35.1 jit_solution(9856078530885807030)
XLA Ops:
  1.9 30.0 %shard_map.95 = (f32[8,2,256]{2,1,0:T(2,128)}, f32[1,1]{1,0:T(1,128)}) custom-call(bf16[1,2,256,256]{3,2,1,0:T(8,128)(2,1)} %states.1, s32[1]{0:T(128)S(6)} %copy.12.ident_hbm, f32[4,256]{1,0:T(4,128)} %gains_hbm.1, bf16[576,256]{1,0:T(8,128)(2,1)} %w1.1, bf16[576,256]{1,0:T(8,128)(2,1)} %w2.1, bf16[8,256]{1,0:T(8,128)(2,1)} %bitcast.2, ...), custom_call_target="tpu_custom_call" | custom-call | flops 1811939328 | bytes 2359296 | tf_op jit(solution)/shard_map/pallas_call | solution.py:417
  32.0 1.3 %copy.14 = f32[8,2,256]{2,1,0:T(2,128)} copy(f32[8,2,256]{2,1,0:T(2,128)} %get-tuple-element.8) | data formatting | bytes 32768

commit v6 on v5

--- a/solution.py
+++ b/solution.py
@@ -11,6 +11,7 @@
 
 MESH = pl.DeviceIdType.MESH
 TAPS = 9
+ROWTAPS = 3
 
 
 def route(members):
@@ -36,16 +37,14 @@
             arrival = {}
             for stage, (i1, i2) in enumerate(offsets):
                 arrival[((p1 - i1) % n1) * u + ((p2 - i2) % n2) * v] = stage
+            deep = ROWTAPS * chans
             need = [
-                max(
-                    arrival[s]
-                    for s in range(t * chans // shard, ((t + 1) * chans - 1) // shard + 1)
-                )
-                for t in range(TAPS)
+                max(arrival[s] for s in range(g * deep // shard, ((g + 1) * deep - 1) // shard + 1))
+                for g in range(ROWTAPS)
             ]
-            order = sorted(range(TAPS), key=lambda t: need[t])
-            codes.append(sum(t * TAPS**i for i, t in enumerate(order)))
-            stages.append([need[t] for t in order])
+            order = sorted(range(ROWTAPS), key=lambda g: need[g])
+            codes.append(sum(g * ROWTAPS**i for i, g in enumerate(order)))
+            stages.append([need[g] for g in order])
     return offsets, codes, np.max(np.array(stages), axis=0).tolist()
 
 
@@ -126,9 +125,9 @@
     def put_shifted(ref, row, lanes, value):
         low = jnp.where(place_ids == 0, 0.0, pltpu.roll(value, 1, 0))
         high = jnp.where(place_ids == cols - 1, 0.0, pltpu.roll(value, cols - 1, 0))
-        ref[0, row, :, lanes] = low.astype(jnp.bfloat16)
-        ref[1, row, :, lanes] = value.astype(jnp.bfloat16)
-        ref[2, row, :, lanes] = high.astype(jnp.bfloat16)
+        for dx, part in enumerate((low, value, high)):
+            place = pl.ds(pl.multiple_of(dx * chans + lanes.start, strip), strip)
+            ref[row, :, place] = part.astype(jnp.bfloat16)
 
     def scale_rows(count, place):
         @pl.loop(0, count * strips)
@@ -289,7 +288,7 @@
 
         def step(i, left_code):
             done = 0
-            for at in range(TAPS):
+            for at in range(ROWTAPS):
                 due = list(range(done, stage_of[at] + 1))
                 done = max(done, stage_of[at] + 1)
                 if due:
@@ -299,14 +298,14 @@
                         for stage in due:
                             stage_waits(w, stage)
 
-            tap = lax.rem(left_code, TAPS)
-            dy, dx = tap // 3, lax.rem(tap, 3)
-            left = field[dx, pl.ds(base + dy, count)].reshape(count * cols, chans)
-            right = buf[pl.ds(pl.multiple_of(tap * chans, 128), chans), :]
+            deep = ROWTAPS * chans
+            dy = lax.rem(left_code, ROWTAPS)
+            left = field[pl.ds(base + dy, count)].reshape(count * cols, deep)
+            right = buf[pl.ds(pl.multiple_of(dy * deep, 128), deep), :]
             total[...] += jnp.dot(left, right, preferred_element_type=jnp.float32)
-            return left_code // TAPS
-
-        lax.fori_loop(0, TAPS, step, code)
+            return left_code // ROWTAPS
+
+        lax.fori_loop(0, ROWTAPS, step, code)
         if w == 0 and n2 == 1:
             for o1 in range(1, n1):
                 arrive(1, o1, 0)
@@ -324,7 +323,7 @@
 
     conv(1, ish, acc2, rows, 0)
 
-    own = sh[1, pl.ds(rows, rows)].reshape(rows * cols, chans).astype(jnp.float32)
+    own = sh[pl.ds(rows, rows), :, pl.ds(chans, chans)].reshape(rows * cols, chans).astype(jnp.float32)
     block = (own + acc2[...]).astype(jnp.bfloat16)
     pred = lax.dot_general(
         head[...], block, (((1,), (1,)), ((), ())), preferred_element_type=jnp.float32
@@ -430,8 +429,8 @@
             pltpu.SMEM((1,), jnp.int32),
             pltpu.VMEM((8, chans), f32),
             pltpu.VMEM((3 * rows, cols, chans), bf16),
-            pltpu.VMEM((3, 3 * rows, cols, chans), bf16),
-            pltpu.VMEM((3, rows + 2, cols, chans), bf16),
+            pltpu.VMEM((3 * rows, cols, ROWTAPS * chans), bf16),
+            pltpu.VMEM((rows + 2, cols, ROWTAPS * chans), bf16),
             pltpu.VMEM((TAPS * chans, chans), bf16),
             pltpu.VMEM((TAPS * chans, chans), bf16),
             pltpu.VMEM(((rows + 2) * cols, chans), f32),

time: 35.4 us -> 34.5 us (0.975)
  Pallas kernels: 30 us -> 29.2 us
    pallas_call x1, Pallas kernels: 30 us -> 29.2 us  [body(): pl.pallas_call(functools.partial(kernel, members, bands), out_shape=(jax....]
where the time goes in v6:
time: 34.5 us; the launch traced here: 34.2 us
  Pallas kernels  29.2 us (85%)
  between operations  3.7 us (11%)
  local copies, waits for them, and re-layouts  1.32 us (4%)
    pallas_call x1, Pallas kernels, body(): pl.pallas_call(functools.partial(kernel, members, bands), out_shape=(jax....  29.2 us
    unnamed x1, local copies, waits for them, and re-layouts  1.32 us

profile of v6, /device:TPU:0, one launch (start us, length us, event | category | flops | bytes accessed | tf_op | source)
XLA Modules:
  0.0 34.2 jit_solution(10406542952041062787)
XLA Ops:
  1.9 29.2 %shard_map.95 = (f32[8,2,256]{2,1,0:T(2,128)}, f32[1,1]{1,0:T(1,128)}) custom-call(bf16[1,2,256,256]{3,2,1,0:T(8,128)(2,1)} %states.1, s32[1]{0:T(128)S(6)} %copy.12.ident_hbm, f32[4,256]{1,0:T(4,128)} %gains_hbm.1, bf16[576,256]{1,0:T(8,128)(2,1)} %w1.1, bf16[576,256]{1,0:T(8,128)(2,1)} %w2.1, bf16[8,256]{1,0:T(8,128)(2,1)} %bitcast.2, ...), custom_call_target="tpu_custom_call" | custom-call | flops 1811939328 | bytes 2359296 | tf_op jit(solution)/shard_map/pallas_call | solution.py:416
  31.1 1.3 %copy.14 = f32[8,2,256]{2,1,0:T(2,128)} copy(f32[8,2,256]{2,1,0:T(2,128)} %get-tuple-element.8) | data formatting | bytes 32768

commit v7 on v6

--- a/solution.py
+++ b/solution.py
@@ -48,14 +48,14 @@
     return offsets, codes, np.max(np.array(stages), axis=0).tolist()
 
 
-def chunk_count(shard):
-    return 2 if shard % 64 == 0 else 1
+def shared_rows(shard, bands):
+    return shard // 9 if shard % 144 == 0 and shard % 32 == 0 and bands % 4 == 0 else 0
 
 
 def kernel(
     members, bands, states, ident_hbm, gains_hbm, w1, w2, head_hbm, target_hbm, first_row_hbm,
     score_ref, mean_ref, ident, gains, head, target, first_row, gain_ref, raw, sh, ish, wb1, wb2, acc, acc2, preds, parts,
-    local_sem, halo_send, halo_recv, leg_send, leg_recv, sib_send, sib_recv,
+    local_sem, halo_send, halo_recv, leg_send, leg_recv, sib_send, sib_recv, plane_send, plane_recv,
     pred_send, pred_recv, part_send, part_recv,
 ):
     rows, cols, chans = states.shape[1:]
@@ -157,12 +157,17 @@
     def back(i1, i2):
         return member_at(lax.rem(p1 - i1 + n1, n1), lax.rem(p2 - i2 + n2, n2))
 
-    chunks = chunk_count(shard)
+    shared = shared_rows(shard, bands)
+    chunks = 2 if shared else 1
+    passed = 3 if shared else 1
+    parity = lax.rem(lat // 2, 2)
+    partner = lat + 2 - 4 * parity
 
     def half(ref, base, which, chunk):
-        if shard % (32 * chunks) == 0:
-            size = shard // (2 * chunks)
-            first = base + which * (shard // 2) + chunk * size
+        if shared:
+            first = base + which * (shard // 2)
+            first += (parity * shared, 2 * shared, (1 - parity) * shared)[chunk]
+            size = (shared, shard // 2 - 2 * shared, shared)[chunk]
             return ref.at[pl.ds(pl.multiple_of(first, 16), size)]
         span = ref.shape[1] // 2
         return ref.at[
@@ -201,6 +206,23 @@
             device_id_type=MESH,
         )
 
+    def plane_copy(w, i1, i2, chunk):
+        buf = (wb1, wb2)[w]
+        place = half(buf, back(i1, i2) * shard, core, chunk)
+        return pltpu.make_async_remote_copy(
+            src_ref=place,
+            dst_ref=place,
+            send_sem=plane_send.at[w, i1, i2],
+            recv_sem=plane_recv.at[w, i1, i2],
+            device_id=(me, partner),
+            device_id_type=MESH,
+        )
+
+    def plane_arrive(w, i1, i2):
+        if shared:
+            plane_copy(w, i1, i2, 2).wait_recv()
+            sib_copy(w, i1, i2, 2).start()
+
     def send_own(w, some):
         for chunk in some:
             for i1 in range(1, n1):
@@ -214,6 +236,8 @@
             if i2 == 0:
                 for j2 in range(1, n2):
                     leg_copy(w, i1, j2, chunk).start()
+            if shared and chunk == 0:
+                plane_copy(w, i1, i2, 0).start()
             sib_copy(w, i1, i2, chunk).start()
 
     def halo_copy(step):
@@ -280,7 +304,10 @@
             for o1, o2 in offsets:
                 if legs(o1, o2) == legs(i1, i2) and o2 > 0:
                     arrive(w, o1, o2)
-        for chunk in range(chunks):
+            for o1, o2 in offsets:
+                if legs(o1, o2) == legs(i1, i2):
+                    plane_arrive(w, o1, o2)
+        for chunk in range(passed):
             sib_copy(w, *((i2, i1) if n2 > 1 else (i1, i2)), chunk).wait_recv()
 
     def conv(w, field, total, count, base):
@@ -396,7 +423,10 @@
         for i1, i2 in offsets[1:]:
             for chunk in range(chunks):
                 leg_copy(w, i1, i2, chunk).wait_send()
+            for chunk in range(passed):
                 sib_copy(w, i1, i2, chunk).wait_send()
+            if shared:
+                plane_copy(w, i1, i2, 0).wait_send()
     for copy in pred_copies + part_copies:
         copy.wait_send()
 
@@ -407,7 +437,6 @@
     fields = head.shape[1]
     args = args[:5] + (head.T,) + args[6:]
     n1, n2 = route(members)
-    chunks = chunk_count(args[3].shape[0])
     hbm = pl.BlockSpec(memory_space=pltpu.HBM)
     vmem = pl.BlockSpec(memory_space=pltpu.VMEM)
     smem = pl.BlockSpec(memory_space=pltpu.SMEM)
@@ -440,10 +469,12 @@
             dma((8,)),
             dma((2,)),
             dma((2,)),
-            dma((2, n1, n2, chunks)),
-            dma((2, n1, n2, chunks)),
-            dma((2, n1, n2, chunks)),
-            dma((2, n1, n2, chunks)),
+            dma((2, n1, n2, 2)),
+            dma((2, n1, n2, 2)),
+            dma((2, n1, n2, 3)),
+            dma((2, n1, n2, 3)),
+            dma((2, n1, n2)),
+            dma((2, n1, n2)),
             dma((members,)),
             dma((members,)),
             dma((bands,)),

time: 34.5 us -> 43.9 us (1.27)
  Pallas kernels: 29.2 us -> 38.6 us
    pallas_call x1, Pallas kernels: 29.2 us -> 38.6 us  [body(): pl.pallas_call(functools.partial(kernel, members, bands), out_shape=(jax....]
where the time goes in v7:
time: 43.9 us; the launch traced here: 43.6 us
  Pallas kernels  38.6 us (88%)
  between operations  3.7 us (8%)
  local copies, waits for them, and re-layouts  1.32 us (3%)
    pallas_call x1, Pallas kernels, body(): pl.pallas_call(functools.partial(kernel, members, bands), out_shape=(jax....  38.6 us
    unnamed x1, local copies, waits for them, and re-layouts  1.32 us

profile of v7, /device:TPU:0, one launch (start us, length us, event | category | flops | bytes accessed | tf_op | source)
XLA Modules:
  0.0 43.6 jit_solution(7656726412431177863)
XLA Ops:
  1.9 38.6 %shard_map.95 = (f32[8,2,256]{2,1,0:T(2,128)}, f32[1,1]{1,0:T(1,128)}) custom-call(bf16[1,2,256,256]{3,2,1,0:T(8,128)(2,1)} %states.1, s32[1]{0:T(128)S(6)} %copy.12.ident_hbm, f32[4,256]{1,0:T(4,128)} %gains_hbm.1, bf16[576,256]{1,0:T(8,128)(2,1)} %w1.1, bf16[576,256]{1,0:T(8,128)(2,1)} %w2.1, bf16[8,256]{1,0:T(8,128)(2,1)} %bitcast.2, ...), custom_call_target="tpu_custom_call" | custom-call | flops 1811939328 | bytes 2359296 | tf_op jit(solution)/shard_map/pallas_call | solution.py:445
  40.5 1.3 %copy.14 = f32[8,2,256]{2,1,0:T(2,128)} copy(f32[8,2,256]{2,1,0:T(2,128)} %get-tuple-element.8) | data formatting | bytes 32768

commit v8 on v6

--- a/solution.py
+++ b/solution.py
@@ -49,7 +49,7 @@
 
 
 def chunk_count(shard):
-    return 2 if shard % 64 == 0 else 1
+    return 1
 
 
 def kernel(
@@ -171,18 +171,10 @@
 
     def leg_copy(w, i1, i2, chunk):
         src, buf = ((w1, wb1), (w2, wb2))[w]
-        if i2 == 0:
-            dest = member_at(lax.rem(p1 + i1, n1), p2)
-            origin, j1 = me, 0
-        else:
-            dest = member_at(p1, lax.rem(p2 + i2, n2))
-            origin, j1 = back(i1, 0), i1
-        source = (
-            half(src, 0, core, chunk) if j1 == 0 else half(buf, origin * shard, core, chunk)
-        )
+        dest = member_at(lax.rem(p1 + i1, n1), lax.rem(p2 + i2, n2))
         return pltpu.make_async_remote_copy(
-            src_ref=source,
-            dst_ref=half(buf, origin * shard, core, chunk),
+            src_ref=half(src, 0, core, chunk),
+            dst_ref=half(buf, me * shard, core, chunk),
             send_sem=leg_send.at[w, i1, i2, chunk],
             recv_sem=leg_recv.at[w, i1, i2, chunk],
             device_id=(dest, lat),
@@ -203,17 +195,12 @@
 
     def send_own(w, some):
         for chunk in some:
-            for i1 in range(1, n1):
-                leg_copy(w, i1, 0, chunk).start()
-            for i2 in range(1, n2):
-                leg_copy(w, 0, i2, chunk).start()
+            for i1, i2 in offsets[1:]:
+                leg_copy(w, i1, i2, chunk).start()
 
     def arrive(w, i1, i2, some=range(chunks)):
         for chunk in some:
             leg_copy(w, i1, i2, chunk).wait_recv()
-            if i2 == 0:
-                for j2 in range(1, n2):
-                    leg_copy(w, i1, j2, chunk).start()
             sib_copy(w, i1, i2, chunk).start()
 
     def halo_copy(step):

time: 34.5 us -> 37 us (1.072)
  Pallas kernels: 29.2 us -> 31.6 us
    pallas_call x1, Pallas kernels: 29.2 us -> 31.6 us  [body(): pl.pallas_call(functools.partial(kernel, members, bands), out_shape=(jax....]
where the time goes in v8:
time: 37 us; the launch traced here: 36.7 us
  Pallas kernels  31.6 us (85%)
  between operations  3.7 us (10%)
  local copies, waits for them, and re-layouts  1.32 us (4%)
    pallas_call x1, Pallas kernels, body(): pl.pallas_call(functools.partial(kernel, members, bands), out_shape=(jax....  31.6 us
    unnamed x1, local copies, waits for them, and re-layouts  1.32 us

profile of v8, /device:TPU:0, one launch (start us, length us, event | category | flops | bytes accessed | tf_op | source)
XLA Modules:
  0.0 36.7 jit_solution(7650746569602488409)
XLA Ops:
  1.9 31.6 %shard_map.95 = (f32[8,2,256]{2,1,0:T(2,128)}, f32[1,1]{1,0:T(1,128)}) custom-call(bf16[1,2,256,256]{3,2,1,0:T(8,128)(2,1)} %states.1, s32[1]{0:T(128)S(6)} %copy.12.ident_hbm, f32[4,256]{1,0:T(4,128)} %gains_hbm.1, bf16[576,256]{1,0:T(8,128)(2,1)} %w1.1, bf16[576,256]{1,0:T(8,128)(2,1)} %w2.1, bf16[8,256]{1,0:T(8,128)(2,1)} %bitcast.2, ...), custom_call_target="tpu_custom_call" | custom-call | flops 1811939328 | bytes 2359296 | tf_op jit(solution)/shard_map/pallas_call | solution.py:403
  33.6 1.3 %copy.14 = f32[8,2,256]{2,1,0:T(2,128)} copy(f32[8,2,256]{2,1,0:T(2,128)} %get-tuple-element.8) | data formatting | bytes 32768

commit v9 on v6

--- a/solution.py
+++ b/solution.py
@@ -98,50 +98,6 @@
     ]
     for copy in small + locals_:
         copy.start()
-    for copy in small:
-        copy.wait()
-
-    lane = lax.broadcasted_iota(jnp.int32, gains.shape, 0)
-    gain = jnp.sum(jnp.where(lane == ident[0], gains[...], 0.0), axis=0, keepdims=True)
-
-    all_rows = rows * bands
-    width = -(-all_rows // 128) * 128
-    ids = lax.broadcasted_iota(jnp.int32, (8, width), 1)
-    area_all = jnp.cos(jnp.pi * (90.0 - 0.1 * (first_row[0] + ids).astype(jnp.float32)) / 180.0)
-
-    def area_sum(chosen):
-        return jnp.sum(jnp.where(chosen, area_all, 0.0)[0:1], axis=1, keepdims=True)
-
-    area_total = area_sum(ids < all_rows)
-    areas = [area_sum(ids == lat * rows + r) for r in range(rows)]
-
-    strip = 128
-    strips = chans // strip
-    place_ids = lax.broadcasted_iota(jnp.int32, (cols, strip), 0)
-
-    def lanes_of(index):
-        return pl.ds(pl.multiple_of(lax.rem(index, strips) * strip, strip), strip)
-
-    def put_shifted(ref, row, lanes, value):
-        low = jnp.where(place_ids == 0, 0.0, pltpu.roll(value, 1, 0))
-        high = jnp.where(place_ids == cols - 1, 0.0, pltpu.roll(value, cols - 1, 0))
-        for dx, part in enumerate((low, value, high)):
-            place = pl.ds(pl.multiple_of(dx * chans + lanes.start, strip), strip)
-            ref[row, :, place] = part.astype(jnp.bfloat16)
-
-    def scale_rows(count, place):
-        @pl.loop(0, count * strips)
-        def _(index):
-            row, lanes = place(index // strips), lanes_of(index)
-            value = raw[row, :, lanes].astype(jnp.float32) * gain_ref[0:1, lanes]
-            put_shifted(sh, row, lanes, value)
-
-    gain_ref[...] = jnp.broadcast_to(gain, gain_ref.shape)
-    locals_[0].wait()
-    scale_rows(rows, lambda r: r + rows)
-    acc[...] = jnp.zeros_like(acc)
-    acc2[...] = jnp.zeros_like(acc2)
-
     pl.semaphore_wait(barrier, members - 1 + bands - 1)
 
     if n2 > 1:
@@ -239,10 +195,54 @@
     def _():
         halo_copy(-1).start()
 
+    for copy in small:
+        copy.wait()
+
+    lane = lax.broadcasted_iota(jnp.int32, gains.shape, 0)
+    gain = jnp.sum(jnp.where(lane == ident[0], gains[...], 0.0), axis=0, keepdims=True)
+
+    all_rows = rows * bands
+    width = -(-all_rows // 128) * 128
+    ids = lax.broadcasted_iota(jnp.int32, (8, width), 1)
+    area_all = jnp.cos(jnp.pi * (90.0 - 0.1 * (first_row[0] + ids).astype(jnp.float32)) / 180.0)
+
+    def area_sum(chosen):
+        return jnp.sum(jnp.where(chosen, area_all, 0.0)[0:1], axis=1, keepdims=True)
+
+    area_total = area_sum(ids < all_rows)
+    areas = [area_sum(ids == lat * rows + r) for r in range(rows)]
+
+    strip = 128
+    strips = chans // strip
+    place_ids = lax.broadcasted_iota(jnp.int32, (cols, strip), 0)
+
+    def lanes_of(index):
+        return pl.ds(pl.multiple_of(lax.rem(index, strips) * strip, strip), strip)
+
+    def put_shifted(ref, row, lanes, value):
+        low = jnp.where(place_ids == 0, 0.0, pltpu.roll(value, 1, 0))
+        high = jnp.where(place_ids == cols - 1, 0.0, pltpu.roll(value, cols - 1, 0))
+        for dx, part in enumerate((low, value, high)):
+            place = pl.ds(pl.multiple_of(dx * chans + lanes.start, strip), strip)
+            ref[row, :, place] = part.astype(jnp.bfloat16)
+
+    def scale_rows(count, place):
+        @pl.loop(0, count * strips)
+        def _(index):
+            row, lanes = place(index // strips), lanes_of(index)
+            value = raw[row, :, lanes].astype(jnp.float32) * gain_ref[0:1, lanes]
+            put_shifted(sh, row, lanes, value)
+
+    gain_ref[...] = jnp.broadcast_to(gain, gain_ref.shape)
+    locals_[0].wait()
+    scale_rows(rows, lambda r: r + rows)
+
     for chunk in range(chunks):
         for i1 in range(1, n1):
             arrive(0, i1, 0, [chunk])
         send_own(1, [chunk])
+    acc[...] = jnp.zeros_like(acc)
+    acc2[...] = jnp.zeros_like(acc2)
 
 
     @pl.when(has_low)

time: 34.5 us -> 34.3 us (level)
  no operation moved by 1% of the time
where the time goes in v9:
time: 34.3 us; the launch traced here: 34 us
  Pallas kernels  29 us (85%)
  between operations  3.7 us (11%)
  local copies, waits for them, and re-layouts  1.32 us (4%)
    pallas_call x1, Pallas kernels, body(): pl.pallas_call(functools.partial(kernel, members, bands), out_shape=(jax....  29 us
    unnamed x1, local copies, waits for them, and re-layouts  1.32 us

profile of v9, /device:TPU:0, one launch (start us, length us, event | category | flops | bytes accessed | tf_op | source)
XLA Modules:
  0.0 34.0 jit_solution(17910118757216783637)
XLA Ops:
  1.9 29.0 %shard_map.95 = (f32[8,2,256]{2,1,0:T(2,128)}, f32[1,1]{1,0:T(1,128)}) custom-call(bf16[1,2,256,256]{3,2,1,0:T(8,128)(2,1)} %states.1, s32[1]{0:T(128)S(6)} %copy.12.ident_hbm, f32[4,256]{1,0:T(4,128)} %gains_hbm.1, bf16[576,256]{1,0:T(8,128)(2,1)} %w1.1, bf16[576,256]{1,0:T(8,128)(2,1)} %w2.1, bf16[8,256]{1,0:T(8,128)(2,1)} %bitcast.2, ...), custom_call_target="tpu_custom_call" | custom-call | flops 1811939328 | bytes 2359296 | tf_op jit(solution)/shard_map/pallas_call | solution.py:416
  30.9 1.3 %copy.14 = f32[8,2,256]{2,1,0:T(2,128)} copy(f32[8,2,256]{2,1,0:T(2,128)} %get-tuple-element.8) | data formatting | bytes 32768

commit v10 on v9

--- a/solution.py
+++ b/solution.py
@@ -274,12 +274,12 @@
             locals_[1 + w].wait()
             return
         if legs(i1, i2) > legs(*offsets[stage - 1]):
+            for o1, o2 in offsets:
+                if legs(o1, o2) == legs(i1, i2) and o2 > 0:
+                    arrive(w, o1, o2)
             if w == 0 and legs(i1, i2) == 2:
                 for o1 in range(1, n1):
                     arrive(1, o1, 0)
-            for o1, o2 in offsets:
-                if legs(o1, o2) == legs(i1, i2) and o2 > 0:
-                    arrive(w, o1, o2)
         for chunk in range(chunks):
             sib_copy(w, *((i2, i1) if n2 > 1 else (i1, i2)), chunk).wait_recv()
 

time: 34.3 us -> 34.1 us (level)
  no operation moved by 1% of the time
where the time goes in v10:
time: 34.1 us; the launch traced here: 33.8 us
  Pallas kernels  28.8 us (84%)
  between operations  3.7 us (11%)
  local copies, waits for them, and re-layouts  1.32 us (4%)
    pallas_call x1, Pallas kernels, body(): pl.pallas_call(functools.partial(kernel, members, bands), out_shape=(jax....  28.8 us
    unnamed x1, local copies, waits for them, and re-layouts  1.32 us

profile of v10, /device:TPU:0, one launch (start us, length us, event | category | flops | bytes accessed | tf_op | source)
XLA Modules:
  0.0 33.8 jit_solution(17803990578830880518)
XLA Ops:
  1.9 28.8 %shard_map.95 = (f32[8,2,256]{2,1,0:T(2,128)}, f32[1,1]{1,0:T(1,128)}) custom-call(bf16[1,2,256,256]{3,2,1,0:T(8,128)(2,1)} %states.1, s32[1]{0:T(128)S(6)} %copy.12.ident_hbm, f32[4,256]{1,0:T(4,128)} %gains_hbm.1, bf16[576,256]{1,0:T(8,128)(2,1)} %w1.1, bf16[576,256]{1,0:T(8,128)(2,1)} %w2.1, bf16[8,256]{1,0:T(8,128)(2,1)} %bitcast.2, ...), custom_call_target="tpu_custom_call" | custom-call | flops 1811939328 | bytes 2359296 | tf_op jit(solution)/shard_map/pallas_call | solution.py:416
  30.7 1.3 %copy.14 = f32[8,2,256]{2,1,0:T(2,128)} copy(f32[8,2,256]{2,1,0:T(2,128)} %get-tuple-element.8) | data formatting | bytes 32768
